TPU v7x, 256 devices: a whole 4x4x8 slice. The times are simulated.
256 devices in a mesh: wide: 16 (over x, y), narrow: 16 (over z, core).
Axes of the slice: x: 4, y: 4, z: 8, core: 2. Of those that a mesh axis runs over, the one named last changes fastest.
Arguments:
- model: float32 [512, 2, 256, 256], P(('wide', 'narrow')), may hold values from -6 to 6
- observed: float32 [512, 2, 256, 256], P(('wide', 'narrow')), may hold values from -6 to 6
- own_weights: float32 [5, 512, 2, 256, 256], P(None, ('wide', 'narrow')), may hold values from -0.1875 to 0.1875
- partner_weights: float32 [5, 512, 2, 256, 256], P(None, ('wide', 'narrow')), may hold values from -0.1875 to 0.1875
Outputs:
- residual: float32 [512, 2, 256, 256], P(('wide', 'narrow'))
- gradient: float32 [512, 2, 256, 256], P(('wide', 'narrow'))
All inputs are finite; a program needn't handle non-finite values.
Results may differ from a plain program's by a relative error of at most 0.0001.
Values sent between devices are 32-bit elements; how exact they have to be, the bound alone decides.
A program may use at most 128 MiB of HBM per device.

v0:
```python
import functools

import jax
import jax.numpy as jnp
from jax import lax
from jax.experimental import pallas as pl
from jax.experimental.pallas import tpu as pltpu
from jax.sharding import PartitionSpec as P

MESH = pl.DeviceIdType.MESH
LEVELS = 5
CHUNKS = 8
DELAYS = (0, 1, 3, 4, 5, 6, 7, 10, 11)
BF16, F32 = jnp.bfloat16, jnp.float32


def split(x):
    high = x.astype(BF16)
    return high, (x - high.astype(F32)).astype(BF16)


def high_low(x):
    high, low = split(x)
    return jnp.concatenate([high, low], axis=0)


def dot(a, b):
    return jnp.dot(a, b, preferred_element_type=F32)


def dot_t(a, b):
    return lax.dot_general(a, b, (((1,), (1,)), ((), ())), preferred_element_type=F32)


def kernel(
    model, observed, own, partner, residual, gradient,
    start, data, own_f32, partner_f32, w_high, w_low,
    state, other, kept, term, carried, res_out, grad_out,
    in_sem, weight_sem, out_sem, send_sem, recv_sem,
):
    rows = model.shape[2]
    k = model.shape[3]
    chunks = state.shape[1]
    size = rows // chunks
    narrow, wide = lax.axis_index("narrow"), lax.axis_index("wide")
    narrow_top, wide_top = lax.axis_size("narrow") // 2, lax.axis_size("wide") // 2
    partners = {
        1: (wide, jnp.bitwise_xor(narrow, 1)),
        2: (wide, jnp.bitwise_xor(narrow, narrow_top)),
        3: (jnp.bitwise_xor(wide, 1), narrow),
        4: (jnp.bitwise_xor(wide, wide_top), narrow),
    }

    copy_in = [
        pltpu.make_async_copy(model, start, in_sem.at[0]),
        pltpu.make_async_copy(observed, data, in_sem.at[1]),
    ]

    def weights_in(level):
        return (
            pltpu.make_async_copy(own.at[level], own_f32.at[level], weight_sem.at[0, level]),
            pltpu.make_async_copy(partner.at[level], partner_f32.at[level], weight_sem.at[1, level]),
        )

    def exchange(level, c, back):
        slot = level - 1
        way = 4 * back + slot
        return pltpu.make_async_remote_copy(
            src_ref=(term if back else state).at[slot, c],
            dst_ref=(carried if back else other).at[slot, c],
            send_sem=send_sem.at[way, c],
            recv_sem=recv_sem.at[way, c],
            device_id=partners[level],
            device_id_type=MESH,
        )

    def copy_out(c, which):
        src, dst = ((res_out, residual), (grad_out, gradient))[which]
        return pltpu.make_async_copy(
            src.at[c], dst.at[:, :, pl.ds(c * size, size), :], out_sem.at[which, c]
        )

    copy_in[0].start()
    for level in range(LEVELS):
        for copy in weights_in(level):
            copy.start()
        if level == 1:
            copy_in[1].start()

    barrier = pltpu.get_barrier_semaphore()
    for level in range(1, LEVELS):
        pl.semaphore_signal(barrier, inc=1, device_id=partners[level], device_id_type=MESH)
    pl.semaphore_wait(barrier, LEVELS - 1)

    def prepare(level):
        for copy in weights_in(level):
            copy.wait()

        @pl.loop(0, 2)
        def _(b):
            for i, source in enumerate((own_f32, partner_f32)):
                for part in range(2):
                    high, low = split(source[level, b, part])
                    place = pl.ds((2 * i + part) * k, k)
                    w_high[level, b, place, :] = high
                    w_low[level, b, place, :] = low

    def forward(level, mine, theirs, b):
        (ur, ui), (vr, vi) = mine, theirs
        real = jnp.concatenate([ur, -ui, vr, -vi], axis=1)
        imag = jnp.concatenate([ui, ur, vi, vr], axis=1)
        high, low = split(jnp.concatenate([real, imag], axis=0))
        both = dot(jnp.concatenate([high, low], axis=0), w_high[level, b])
        out = both[: 2 * size] + both[2 * size :] + dot(high, w_low[level, b])
        return out[:size], out[size:]

    def adjoint_side(gr, gi):
        first = jnp.concatenate([gr, gi], axis=0)
        second = jnp.concatenate([gi, -gr], axis=0)
        return split(jnp.concatenate([first, second], axis=1))

    def adjoint(level, which, side, b):
        high, low = side

        def weight(w):
            return jnp.concatenate(
                [w[level, b, pl.ds((2 * which + part) * k, k), :] for part in range(2)], axis=1
            )

        both = dot_t(jnp.concatenate([high, low], axis=0), weight(w_high))
        out = both[: 2 * size] + both[2 * size :] + dot_t(high, weight(w_low))
        return out[:size], out[size:]

    def put(ref, index, value):
        for part in range(2):
            ref[(*index, part)] = value[part]

    def back_level(level, c, grads):
        sides = [adjoint_side(*g) for g in grads]
        for b in range(2):
            put(term, (level - 1, c, b), adjoint(level, 1, sides[b], b))
        exchange(level, c, 1).start()
        for b in range(2):
            put(kept, (level - 1, c, b), adjoint(level, 0, sides[b], b))

    def arrived(level, c):
        exchange(level, c, 1).wait_recv()
        return [
            [kept[level - 1, c, b, part] + carried[level - 1, c, b, part] for part in range(2)]
            for b in range(2)
        ]

    def first(c):
        @pl.when(c == 0)
        def _():
            copy_in[0].wait()
            prepare(0)

        at = pl.ds(pl.multiple_of(c * size, size), size)
        boxes = [[start[b, part, at, :] for part in range(2)] for b in range(2)]
        for b in range(2):
            put(state, (0, c, b), forward(0, boxes[b], boxes[1 - b], b))
        exchange(1, c, 0).start()

    def middle(level, c):
        @pl.when(c == 0)
        def _():
            prepare(level)

        exchange(level, c, 0).wait_recv()
        slot = level - 1
        for b in range(2):
            mine, theirs = ([ref[slot, c, b, part] for part in range(2)] for ref in (state, other))
            put(state, (slot + 1, c, b), forward(level, mine, theirs, b))
        exchange(level + 1, c, 0).start()

    def turn(c):
        @pl.when(c == 0)
        def _():
            prepare(4)
            copy_in[1].wait()

        exchange(4, c, 0).wait_recv()
        at = pl.ds(pl.multiple_of(c * size, size), size)
        grads = []
        for b in range(2):
            mine, theirs = ([ref[3, c, b, part] for part in range(2)] for ref in (state, other))
            out = forward(4, mine, theirs, b)
            grads.append([out[part] - data[b, part, at, :] for part in range(2)])
            put(res_out, (c, b), grads[b])
        back_level(4, c, grads)
        copy_out(c, 0).start()

    def last(c):
        sides = [adjoint_side(*g) for g in arrived(1, c)]
        for b in range(2):
            mine = adjoint(0, 0, sides[b], b)
            theirs = adjoint(0, 1, sides[1 - b], 1 - b)
            put(grad_out, (c, b), [mine[part] + theirs[part] for part in range(2)])
        copy_out(c, 1).start()

    tasks = [
        first,
        functools.partial(middle, 1),
        functools.partial(middle, 2),
        functools.partial(middle, 3),
        turn,
        lambda c: back_level(3, c, arrived(4, c)),
        lambda c: back_level(2, c, arrived(3, c)),
        lambda c: back_level(1, c, arrived(2, c)),
        last,
    ]

    @pl.loop(0, chunks + DELAYS[-1])
    def _(step):
        for task, delay in zip(tasks, DELAYS):
            c = step - delay
            pl.when(jnp.logical_and(c >= 0, c < chunks))(functools.partial(task, c))

    @pl.loop(0, chunks)
    def _(c):
        for back in range(2):
            for level in range(1, LEVELS):
                exchange(level, c, back).wait_send()
        for which in range(2):
            copy_out(c, which).wait()


def shards(model, observed, own, partner):
    boxes, parts, rows, k = model.shape
    size = rows // CHUNKS
    chunked = (CHUNKS, boxes, parts, size, k)
    whole = pltpu.VMEM((LEVELS - 1, *chunked), F32)
    flops = 2 * 2 * LEVELS * boxes * 8 * rows * k * k * 3
    return pl.pallas_call(
        kernel,
        out_shape=[jax.ShapeDtypeStruct(model.shape, F32)] * 2,
        in_specs=[pl.BlockSpec(memory_space=pltpu.HBM)] * 4,
        out_specs=[pl.BlockSpec(memory_space=pltpu.HBM)] * 2,
        scratch_shapes=[
            pltpu.VMEM(model.shape, F32),
            pltpu.VMEM(model.shape, F32),
            pltpu.VMEM(own.shape, F32),
            pltpu.VMEM(own.shape, F32),
            pltpu.VMEM((LEVELS, boxes, 4 * k, k), BF16),
            pltpu.VMEM((LEVELS, boxes, 4 * k, k), BF16),
            whole, whole, whole, whole, whole,
            pltpu.VMEM(chunked, F32),
            pltpu.VMEM(chunked, F32),
            pltpu.SemaphoreType.DMA((2,)),
            pltpu.SemaphoreType.DMA((2, LEVELS)),
            pltpu.SemaphoreType.DMA((2, CHUNKS)),
            pltpu.SemaphoreType.DMA((8, CHUNKS)),
            pltpu.SemaphoreType.DMA((8, CHUNKS)),
        ],
        compiler_params=pltpu.CompilerParams(
            collective_id=0, has_side_effects=True, vmem_limit_bytes=58 * 2**20
        ),
        cost_estimate=pl.CostEstimate(flops=flops, bytes_accessed=14 * 2**20, transcendentals=0),
    )(model, observed, own, partner)


def solution(mesh):
    boxes = P(("wide", "narrow"), None, None, None)
    weights = P(None, ("wide", "narrow"), None, None, None)
    return jax.shard_map(
        shards,
        mesh=mesh,
        in_specs=(boxes, boxes, weights, weights),
        out_specs=(boxes, boxes),
        check_vma=False,
    )
```

profile of v0, /device:TPU:49, one launch (start us, length us, event | category | flops | bytes accessed | tf_op | source)
XLA Modules:
  0.0 113.3 jit_solution(9355212504151978925)
XLA Ops:
  0.6 108.1 %shard_map.59 = (f32[2,2,256,256]{3,2,1,0:T(8,128)}, f32[2,2,256,256]{3,2,1,0:T(8,128)}) custom-call(f32[2,2,256,256]{3,2,1,0:T(8,128)} %model.1, f32[2,2,256,256]{3,2,1,0:T(8,128)} %observed.1, f32[5,2,2,256,256]{4,3,2,1,0:T(8,128)} %own.1, f32[5,2,2,256,256]{4,3,2,1,0:T(8,128)} %partner.1), custom_call_target="tpu_custom_call" | custom-call | flops 16106127360 | bytes 14680064 | tf_op jit(solution)/shard_map/pallas_call | solution.py:235
  108.8 2.3 %copy.8 = f32[2,2,256,256]{3,2,1,0:T(8,128)} copy(f32[2,2,256,256]{3,2,1,0:T(8,128)} %get-tuple-element.4) | data formatting | bytes 2097152
  111.1 2.3 %copy.9 = f32[2,2,256,256]{3,2,1,0:T(8,128)} copy(f32[2,2,256,256]{3,2,1,0:T(8,128)} %get-tuple-element.5) | data formatting | bytes 2097152
where the time goes:
time: 115 us; the launch traced here: 113 us
  Pallas kernels  108 us (94%)
  local copies, waits for them, and re-layouts  4.57 us (4%)
    pallas_call x1, Pallas kernels, shards(): pl.pallas_call(kernel, out_shape=[jax.ShapeDtypeStruct(model.shape, F32)]...  108 us
    unnamed x2, local copies, waits for them, and re-layouts  4.57 us

commit v1 on v0

--- a/solution.py
+++ b/solution.py
@@ -35,8 +35,8 @@
 def kernel(
     model, observed, own, partner, residual, gradient,
     start, data, own_f32, partner_f32, w_high, w_low,
-    state, other, kept, term, carried, res_out, grad_out,
-    in_sem, weight_sem, out_sem, send_sem, recv_sem,
+    state, other, kept, term, carried,
+    in_sem, weight_sem, send_sem, recv_sem,
 ):
     rows = model.shape[2]
     k = model.shape[3]
@@ -74,23 +74,13 @@
             device_id_type=MESH,
         )
 
-    def copy_out(c, which):
-        src, dst = ((res_out, residual), (grad_out, gradient))[which]
-        return pltpu.make_async_copy(
-            src.at[c], dst.at[:, :, pl.ds(c * size, size), :], out_sem.at[which, c]
-        )
-
     copy_in[0].start()
-    for level in range(LEVELS):
-        for copy in weights_in(level):
-            copy.start()
-        if level == 1:
-            copy_in[1].start()
+    for copy in weights_in(0):
+        copy.start()
 
     barrier = pltpu.get_barrier_semaphore()
     for level in range(1, LEVELS):
         pl.semaphore_signal(barrier, inc=1, device_id=partners[level], device_id_type=MESH)
-    pl.semaphore_wait(barrier, LEVELS - 1)
 
     def prepare(level):
         for copy in weights_in(level):
@@ -151,15 +141,15 @@
         ]
 
     def first(c):
+        at = pl.ds(pl.multiple_of(c * size, size), size)
+        boxes = [[start[b, part, at, :] for part in range(2)] for b in range(2)]
+        for b in range(2):
+            put(state, (0, c, b), forward(0, boxes[b], boxes[1 - b], b))
+
         @pl.when(c == 0)
         def _():
-            copy_in[0].wait()
-            prepare(0)
-
-        at = pl.ds(pl.multiple_of(c * size, size), size)
-        boxes = [[start[b, part, at, :] for part in range(2)] for b in range(2)]
-        for b in range(2):
-            put(state, (0, c, b), forward(0, boxes[b], boxes[1 - b], b))
+            pl.semaphore_wait(barrier, LEVELS - 1)
+
         exchange(1, c, 0).start()
 
     def middle(level, c):
@@ -187,17 +177,18 @@
             mine, theirs = ([ref[3, c, b, part] for part in range(2)] for ref in (state, other))
             out = forward(4, mine, theirs, b)
             grads.append([out[part] - data[b, part, at, :] for part in range(2)])
-            put(res_out, (c, b), grads[b])
+            for part in range(2):
+                residual[b, part, at, :] = grads[b][part]
         back_level(4, c, grads)
-        copy_out(c, 0).start()
 
     def last(c):
         sides = [adjoint_side(*g) for g in arrived(1, c)]
+        at = pl.ds(pl.multiple_of(c * size, size), size)
         for b in range(2):
             mine = adjoint(0, 0, sides[b], b)
             theirs = adjoint(0, 1, sides[1 - b], 1 - b)
-            put(grad_out, (c, b), [mine[part] + theirs[part] for part in range(2)])
-        copy_out(c, 1).start()
+            for part in range(2):
+                gradient[b, part, at, :] = mine[part] + theirs[part]
 
     tasks = [
         first,
@@ -211,6 +202,13 @@
         last,
     ]
 
+    copy_in[0].wait()
+    prepare(0)
+    for level in range(1, LEVELS):
+        for copy in weights_in(level):
+            copy.start()
+    copy_in[1].start()
+
     @pl.loop(0, chunks + DELAYS[-1])
     def _(step):
         for task, delay in zip(tasks, DELAYS):
@@ -222,8 +220,6 @@
         for back in range(2):
             for level in range(1, LEVELS):
                 exchange(level, c, back).wait_send()
-        for which in range(2):
-            copy_out(c, which).wait()
 
 
 def shards(model, observed, own, partner):
@@ -236,7 +232,7 @@
         kernel,
         out_shape=[jax.ShapeDtypeStruct(model.shape, F32)] * 2,
         in_specs=[pl.BlockSpec(memory_space=pltpu.HBM)] * 4,
-        out_specs=[pl.BlockSpec(memory_space=pltpu.HBM)] * 2,
+        out_specs=[pl.BlockSpec(memory_space=pltpu.VMEM)] * 2,
         scratch_shapes=[
             pltpu.VMEM(model.shape, F32),
             pltpu.VMEM(model.shape, F32),
@@ -245,16 +241,13 @@
             pltpu.VMEM((LEVELS, boxes, 4 * k, k), BF16),
             pltpu.VMEM((LEVELS, boxes, 4 * k, k), BF16),
             whole, whole, whole, whole, whole,
-            pltpu.VMEM(chunked, F32),
-            pltpu.VMEM(chunked, F32),
             pltpu.SemaphoreType.DMA((2,)),
             pltpu.SemaphoreType.DMA((2, LEVELS)),
-            pltpu.SemaphoreType.DMA((2, CHUNKS)),
             pltpu.SemaphoreType.DMA((8, CHUNKS)),
             pltpu.SemaphoreType.DMA((8, CHUNKS)),
         ],
         compiler_params=pltpu.CompilerParams(
-            collective_id=0, has_side_effects=True, vmem_limit_bytes=58 * 2**20
+            collective_id=0, has_side_effects=True, vmem_limit_bytes=51 * 2**20
         ),
         cost_estimate=pl.CostEstimate(flops=flops, bytes_accessed=14 * 2**20, transcendentals=0),
     )(model, observed, own, partner)

time: 115 us -> 111 us (0.965); the launches traced: 113 us -> 111 us
  local copies, waits for them, and re-layouts: 4.57 us -> 1.94 us
    unnamed x2, local copies, waits for them, and re-layouts: 4.57 us -> 1.94 us
where the time goes in v1:
time: 111 us
  Pallas kernels  109 us (98%)
  local copies, waits for them, and re-layouts  1.94 us (2%)
    pallas_call x1, Pallas kernels, shards(): pl.pallas_call(kernel, out_shape=[jax.ShapeDtypeStruct(model.shape, F32)]...  109 us

profile of v1, /device:TPU:49, one launch (start us, length us, event | category | flops | bytes accessed | tf_op | source)
XLA Modules:
  0.0 111.3 jit_solution(13866038982027738632)
XLA Ops:
  0.6 108.7 %shard_map.59 = (f32[2,2,256,256]{3,2,1,0:T(8,128)S(1)}, f32[2,2,256,256]{3,2,1,0:T(8,128)S(1)}) custom-call(f32[2,2,256,256]{3,2,1,0:T(8,128)} %model.1, f32[2,2,256,256]{3,2,1,0:T(8,128)} %observed.1, f32[5,2,2,256,256]{4,3,2,1,0:T(8,128)} %own.1, f32[5,2,2,256,256]{4,3,2,1,0:T(8,128)} %partner.1), custom_call_target="tpu_custom_call" | custom-call | flops 16106127360 | bytes 14680064 | tf_op jit(solution)/shard_map/pallas_call | solution.py:231
  109.4 1.0 copy.8
  110.3 1.0 copy.9

commit v2 on v1

--- a/solution.py
+++ b/solution.py
@@ -11,6 +11,7 @@
 LEVELS = 5
 CHUNKS = 8
 DELAYS = (0, 1, 3, 4, 5, 6, 7, 10, 11)
+AHEAD = 3
 BF16, F32 = jnp.bfloat16, jnp.float32
 
 
@@ -36,7 +37,7 @@
     model, observed, own, partner, residual, gradient,
     start, data, own_f32, partner_f32, w_high, w_low,
     state, other, kept, term, carried,
-    in_sem, weight_sem, send_sem, recv_sem,
+    in_sem, weight_sem, send_sem, recv_sem, pace_sem,
 ):
     rows = model.shape[2]
     k = model.shape[3]
@@ -51,6 +52,8 @@
         4: (jnp.bitwise_xor(wide, wide_top), narrow),
     }
 
+    neighbour = (wide, jnp.bitwise_xor(narrow, 2))
+
     copy_in = [
         pltpu.make_async_copy(model, start, in_sem.at[0]),
         pltpu.make_async_copy(observed, data, in_sem.at[1]),
@@ -81,6 +84,7 @@
     barrier = pltpu.get_barrier_semaphore()
     for level in range(1, LEVELS):
         pl.semaphore_signal(barrier, inc=1, device_id=partners[level], device_id_type=MESH)
+    pl.semaphore_signal(barrier, inc=1, device_id=neighbour, device_id_type=MESH)
 
     def prepare(level):
         for copy in weights_in(level):
@@ -148,7 +152,7 @@
 
         @pl.when(c == 0)
         def _():
-            pl.semaphore_wait(barrier, LEVELS - 1)
+            pl.semaphore_wait(barrier, LEVELS)
 
         exchange(1, c, 0).start()
 
@@ -158,10 +162,17 @@
             prepare(level)
 
         exchange(level, c, 0).wait_recv()
+        if level == 2:
+            pl.semaphore_signal(pace_sem, inc=1, device_id=neighbour, device_id_type=MESH)
         slot = level - 1
         for b in range(2):
             mine, theirs = ([ref[slot, c, b, part] for part in range(2)] for ref in (state, other))
             put(state, (slot + 1, c, b), forward(level, mine, theirs, b))
+        if level == 1:
+            @pl.when(c >= AHEAD)
+            def _():
+                pl.semaphore_wait(pace_sem, 1)
+
         exchange(level + 1, c, 0).start()
 
     def turn(c):
@@ -215,11 +226,24 @@
             c = step - delay
             pl.when(jnp.logical_and(c >= 0, c < chunks))(functools.partial(task, c))
 
+    pl.semaphore_wait(pace_sem, min(AHEAD, chunks))
+
     @pl.loop(0, chunks)
     def _(c):
         for back in range(2):
             for level in range(1, LEVELS):
                 exchange(level, c, back).wait_send()
+
+
+def write_back(residual, gradient, residual_out, gradient_out, sem):
+    copies = [
+        pltpu.make_async_copy(source, target, sem.at[i])
+        for i, (source, target) in enumerate(((residual, residual_out), (gradient, gradient_out)))
+    ]
+    for copy in copies:
+        copy.start()
+    for copy in copies:
+        copy.wait()
 
 
 def shards(model, observed, own, partner):
@@ -228,7 +252,7 @@
     chunked = (CHUNKS, boxes, parts, size, k)
     whole = pltpu.VMEM((LEVELS - 1, *chunked), F32)
     flops = 2 * 2 * LEVELS * boxes * 8 * rows * k * k * 3
-    return pl.pallas_call(
+    results = pl.pallas_call(
         kernel,
         out_shape=[jax.ShapeDtypeStruct(model.shape, F32)] * 2,
         in_specs=[pl.BlockSpec(memory_space=pltpu.HBM)] * 4,
@@ -245,12 +269,22 @@
             pltpu.SemaphoreType.DMA((2, LEVELS)),
             pltpu.SemaphoreType.DMA((8, CHUNKS)),
             pltpu.SemaphoreType.DMA((8, CHUNKS)),
+            pltpu.SemaphoreType.REGULAR,
         ],
         compiler_params=pltpu.CompilerParams(
             collective_id=0, has_side_effects=True, vmem_limit_bytes=51 * 2**20
         ),
         cost_estimate=pl.CostEstimate(flops=flops, bytes_accessed=14 * 2**20, transcendentals=0),
     )(model, observed, own, partner)
+    return pl.pallas_call(
+        write_back,
+        out_shape=[jax.ShapeDtypeStruct(model.shape, F32)] * 2,
+        in_specs=[pl.BlockSpec(memory_space=pl.ANY)] * 2,
+        out_specs=[pl.BlockSpec(memory_space=pltpu.HBM)] * 2,
+        scratch_shapes=[pltpu.SemaphoreType.DMA((2,))],
+        compiler_params=pltpu.CompilerParams(vmem_limit_bytes=2**20),
+        cost_estimate=pl.CostEstimate(flops=0, bytes_accessed=4 * 2**20, transcendentals=0),
+    )(*results)
 
 
 def solution(mesh):

time: 111 us -> 110 us (level)
  local copies, waits for them, and re-layouts: 1.94 us -> 0 us
    unnamed x2 -> x0, local copies, waits for them, and re-layouts: 1.94 us -> none
    pallas_call x0 -> x1, Pallas kernels: none -> 1.33 us  [shards(): pl.pallas_call(write_back, out_shape=[jax.ShapeDtypeStruct(model.shape, F...]
where the time goes in v2:
time: 110 us
  Pallas kernels  109 us (99%)
    pallas_call x1, Pallas kernels, shards(): pl.pallas_call(kernel, out_shape=[jax.ShapeDtypeStruct(model.shape, F32)]...  108 us

profile of v2, /device:TPU:49, one launch (start us, length us, event | category | flops | bytes accessed | tf_op | source)
XLA Modules:
  0.0 109.8 jit_solution(9082493083240862056)
XLA Ops:
  0.6 107.8 %shard_map.59 = (f32[2,2,256,256]{3,2,1,0:T(8,128)S(1)}, f32[2,2,256,256]{3,2,1,0:T(8,128)S(1)}) custom-call(f32[2,2,256,256]{3,2,1,0:T(8,128)} %model.1, f32[2,2,256,256]{3,2,1,0:T(8,128)} %observed.1, f32[5,2,2,256,256]{4,3,2,1,0:T(8,128)} %own.1, f32[5,2,2,256,256]{4,3,2,1,0:T(8,128)} %partner.1), custom_call_target="tpu_custom_call" | custom-call | flops 16106127360 | bytes 14680064 | tf_op jit(solution)/shard_map/pallas_call | solution.py:255
  108.4 1.3 %shard_map.60 = (f32[2,2,256,256]{3,2,1,0:T(8,128)}, f32[2,2,256,256]{3,2,1,0:T(8,128)}) custom-call(f32[2,2,256,256]{3,2,1,0:T(8,128)S(1)} %get-tuple-element.4.residual, f32[2,2,256,256]{3,2,1,0:T(8,128)S(1)} %get-tuple-element.5.gradient), custom_call_target="tpu_custom_call" | custom-call | bytes 4194304 | tf_op jit(solution)/shard_map/pallas_call | solution.py:279

commit v3 on v2

--- a/solution.py
+++ b/solution.py
@@ -59,11 +59,11 @@
         pltpu.make_async_copy(observed, data, in_sem.at[1]),
     ]
 
-    def weights_in(level):
-        return (
-            pltpu.make_async_copy(own.at[level], own_f32.at[level], weight_sem.at[0, level]),
-            pltpu.make_async_copy(partner.at[level], partner_f32.at[level], weight_sem.at[1, level]),
-        )
+    def weights_in(level, b):
+        return [
+            pltpu.make_async_copy(source.at[level, b], target.at[level, b], weight_sem.at[i, level, b])
+            for i, (source, target) in enumerate(((own, own_f32), (partner, partner_f32)))
+        ]
 
     def exchange(level, c, back):
         slot = level - 1
@@ -77,8 +77,7 @@
             device_id_type=MESH,
         )
 
-    copy_in[0].start()
-    for copy in weights_in(0):
+    for copy in [*weights_in(0, 0), copy_in[0], *weights_in(0, 1)]:
         copy.start()
 
     barrier = pltpu.get_barrier_semaphore()
@@ -87,11 +86,9 @@
     pl.semaphore_signal(barrier, inc=1, device_id=neighbour, device_id_type=MESH)
 
     def prepare(level):
-        for copy in weights_in(level):
-            copy.wait()
-
-        @pl.loop(0, 2)
-        def _(b):
+        for b in range(2):
+            for copy in weights_in(level, b):
+                copy.wait()
             for i, source in enumerate((own_f32, partner_f32)):
                 for part in range(2):
                     high, low = split(source[level, b, part])
@@ -213,10 +210,10 @@
         last,
     ]
 
+    prepare(0)
     copy_in[0].wait()
-    prepare(0)
     for level in range(1, LEVELS):
-        for copy in weights_in(level):
+        for copy in [*weights_in(level, 0), *weights_in(level, 1)]:
             copy.start()
     copy_in[1].start()
 
@@ -266,7 +263,7 @@
             pltpu.VMEM((LEVELS, boxes, 4 * k, k), BF16),
             whole, whole, whole, whole, whole,
             pltpu.SemaphoreType.DMA((2,)),
-            pltpu.SemaphoreType.DMA((2, LEVELS)),
+            pltpu.SemaphoreType.DMA((2, LEVELS, 2)),
             pltpu.SemaphoreType.DMA((8, CHUNKS)),
             pltpu.SemaphoreType.DMA((8, CHUNKS)),
             pltpu.SemaphoreType.REGULAR,

time: 110 us -> 110 us (level)
  no operation moved by 1% of the time
where the time goes in v3:
time: 110 us
  Pallas kernels  109 us (99%)
    pallas_call x1, Pallas kernels, shards(): pl.pallas_call(kernel, out_shape=[jax.ShapeDtypeStruct(model.shape, F32)]...  108 us

profile of v3, /device:TPU:49, one launch (start us, length us, event | category | flops | bytes accessed | tf_op | source)
XLA Modules:
  0.0 109.8 jit_solution(16215994262346697529)
XLA Ops:
  0.6 107.9 %shard_map.59 = (f32[2,2,256,256]{3,2,1,0:T(8,128)S(1)}, f32[2,2,256,256]{3,2,1,0:T(8,128)S(1)}) custom-call(f32[2,2,256,256]{3,2,1,0:T(8,128)} %model.1, f32[2,2,256,256]{3,2,1,0:T(8,128)} %observed.1, f32[5,2,2,256,256]{4,3,2,1,0:T(8,128)} %own.1, f32[5,2,2,256,256]{4,3,2,1,0:T(8,128)} %partner.1), custom_call_target="tpu_custom_call" | custom-call | flops 16106127360 | bytes 14680064 | tf_op jit(solution)/shard_map/pallas_call | solution.py:252
  108.5 1.3 %shard_map.60 = (f32[2,2,256,256]{3,2,1,0:T(8,128)}, f32[2,2,256,256]{3,2,1,0:T(8,128)}) custom-call(f32[2,2,256,256]{3,2,1,0:T(8,128)S(1)} %get-tuple-element.4.residual, f32[2,2,256,256]{3,2,1,0:T(8,128)S(1)} %get-tuple-element.5.gradient), custom_call_target="tpu_custom_call" | custom-call | bytes 4194304 | tf_op jit(solution)/shard_map/pallas_call | solution.py:276

commit v4 on v2

--- a/solution.py
+++ b/solution.py
@@ -193,6 +193,9 @@
         back_level(4, c, grads)
 
     def last(c):
+        for back in range(2):
+            for level in range(1, LEVELS):
+                exchange(level, c, back).wait_send()
         sides = [adjoint_side(*g) for g in arrived(1, c)]
         at = pl.ds(pl.multiple_of(c * size, size), size)
         for b in range(2):
@@ -227,12 +230,6 @@
             pl.when(jnp.logical_and(c >= 0, c < chunks))(functools.partial(task, c))
 
     pl.semaphore_wait(pace_sem, min(AHEAD, chunks))
-
-    @pl.loop(0, chunks)
-    def _(c):
-        for back in range(2):
-            for level in range(1, LEVELS):
-                exchange(level, c, back).wait_send()
 
 
 def write_back(residual, gradient, residual_out, gradient_out, sem):

time: 110 us -> 110 us (level)
  no operation moved by 1% of the time
where the time goes in v4:
time: 110 us
  Pallas kernels  109 us (99%)
    pallas_call x1, Pallas kernels, shards(): pl.pallas_call(kernel, out_shape=[jax.ShapeDtypeStruct(model.shape, F32)]...  108 us

profile of v4, /device:TPU:49, one launch (start us, length us, event | category | flops | bytes accessed | tf_op | source)
XLA Modules:
  0.0 109.7 jit_solution(8517891545583656604)
XLA Ops:
  0.6 107.7 %shard_map.59 = (f32[2,2,256,256]{3,2,1,0:T(8,128)S(1)}, f32[2,2,256,256]{3,2,1,0:T(8,128)S(1)}) custom-call(f32[2,2,256,256]{3,2,1,0:T(8,128)} %model.1, f32[2,2,256,256]{3,2,1,0:T(8,128)} %observed.1, f32[5,2,2,256,256]{4,3,2,1,0:T(8,128)} %own.1, f32[5,2,2,256,256]{4,3,2,1,0:T(8,128)} %partner.1), custom_call_target="tpu_custom_call" | custom-call | flops 16106127360 | bytes 14680064 | tf_op jit(solution)/shard_map/pallas_call | solution.py:252
  108.3 1.3 %shard_map.60 = (f32[2,2,256,256]{3,2,1,0:T(8,128)}, f32[2,2,256,256]{3,2,1,0:T(8,128)}) custom-call(f32[2,2,256,256]{3,2,1,0:T(8,128)S(1)} %get-tuple-element.4.residual, f32[2,2,256,256]{3,2,1,0:T(8,128)S(1)} %get-tuple-element.5.gradient), custom_call_target="tpu_custom_call" | custom-call | bytes 4194304 | tf_op jit(solution)/shard_map/pallas_call | solution.py:276
